TPU v7x, 32 devices: a whole 2x2x4 slice. The times are simulated.
32 devices in a mesh: dp: 16 (over z, y, core), tensor: 2 (over x).
Axes of the slice: x: 2, y: 2, z: 4, core: 2. Of those that a mesh axis runs over, the one named last changes fastest.
Arguments:
- tokens: bfloat16 [8192, 3072], P('dp', 'tensor'), may hold values from -6 to 6
- w_in: bfloat16 [3072, 3072], P('dp', 'tensor'), may hold values from -0.109375 to 0.109375
- cotangent: bfloat16 [8192, 3072], P('dp', 'tensor'), may hold values from -6 to 6
Outputs:
- hidden: bfloat16 [8192, 3072], P('dp', 'tensor')
- x_grad: bfloat16 [8192, 3072], P('dp', 'tensor')
- w_grad: bfloat16 [3072, 3072], P('dp', 'tensor')
All inputs are finite; a program needn't handle non-finite values.
Results may differ from a plain program's by a relative error of at most 0.028.
Values may be sent and summed in bfloat16 or wider, within the bound.
A program may use at most 128 MiB of HBM per device.

v0:
```python
import jax
import jax.numpy as jnp
from jax import lax
from jax.sharding import PartitionSpec as P


def gelu_tanh(values):
    return jax.nn.gelu(values, approximate=True)


def on_device(tokens, w_in, cotangent):
    weights_all = lax.all_gather(w_in, "dp", axis=0, tiled=True)
    gathered = lax.all_gather(tokens, "tensor", axis=1, tiled=True)
    preact = jnp.dot(gathered, weights_all, preferred_element_type=jnp.float32)
    hidden = gelu_tanh(preact).astype(jnp.bfloat16)
    pull_back = jax.vjp(gelu_tanh, preact)[1]
    pre_grad = pull_back(cotangent.astype(jnp.float32))[0].astype(jnp.bfloat16)
    product = lax.dot_general(
        pre_grad, weights_all, (((1,), (1,)), ((), ())), preferred_element_type=jnp.float32
    )
    x_grad = lax.psum_scatter(
        product.astype(jnp.bfloat16), "tensor", scatter_dimension=1, tiled=True
    )
    w_grad = lax.psum_scatter(
        lax.dot_general(
            gathered, pre_grad, (((0,), (0,)), ((), ())), preferred_element_type=jnp.float32
        ).astype(jnp.bfloat16),
        "dp",
        scatter_dimension=0,
        tiled=True,
    )
    return (hidden, x_grad, w_grad)


def solution(mesh):
    in_specs = (P("dp", "tensor"), P("dp", "tensor"), P("dp", "tensor"))
    out_specs = (P("dp", "tensor"), P("dp", "tensor"), P("dp", "tensor"))
    return jax.shard_map(
        on_device, mesh=mesh, in_specs=in_specs, out_specs=out_specs, check_vma=False
    )
```

profile of v0, /device:TPU:0, one launch (start us, length us, event | category | flops | bytes accessed | tf_op | source)
XLA Modules:
  0.0 326.2 jit_solution(13113354783346358217)
XLA Ops:
  7.2 0.0 all-gather.3.cloned.1.call-start
  7.2 0.7 all-gather.3.cloned.1.call-update
  7.9 0.0 all-gather.5.cloned.1.call-start
  7.9 0.7 all-gather.5.cloned.1.call-update
  8.6 0.0 copy-start.2
  8.7 0.0 reduce-scatter.5.cloned.1.call-start
  8.7 48.5 %all-gather.3.cloned.1.call-done = bf16[512,3072]{1,0:T(8,128)(2,1)} async-done(((bf16[512,1536]{1,0:T(8,128)(2,1)}), bf16[512,3072]{1,0:T(8,128)(2,1)}) %all-gather.3.cloned.1.call-update) | async-done | bytes 3145744 | tf_op jit(solution)/shard_map/all_gather | solution.py:13
  57.2 83.8 %all-gather.5.cloned.1.call-done = bf16[3072,1536]{1,0:T(8,128)(2,1)} async-done(((bf16[192,1536]{1,0:T(8,128)(2,1)}), bf16[3072,1536]{1,0:T(8,128)(2,1)}) %all-gather.5.cloned.1.call-update) | async-done | bytes 9437200 | tf_op jit(solution)/shard_map/all_gather | solution.py:12
  141.0 0.0 copy-start
  141.0 11.0 %multiply_convert_fusion = (bf16[512,1536]{1,0:T(8,128)(2,1)}, f32[512,1536]{1,0:T(8,128)S(1)}) fusion(bf16[512,3072]{1,0:T(8,128)(2,1)} %all-gather.3.cloned.1.call-done, bf16[3072,1536]{1,0:T(8,128)(2,1)} %all-gather.5.cloned.1.call-done), kind=kOutput, calls=%fused_computation.17 | convolution fusion | flops 4838916096 | bytes 17301504 | tf_op jit(solution)/shard_map/dot_general | solution.py:14
  152.0 0.0 copy-start.3
  152.0 1.6 copy-done.3
  153.6 0.0 copy-done.2
  153.6 0.0 copy-done
  153.6 7.9 %convolution_convert_fusion.1 = bf16[512,3072]{1,0:T(8,128)(2,1)} fusion(bf16[3072,1536]{1,0:T(8,128)(2,1)S(1)} %copy-done, bf16[512,1536]{1,0:T(8,128)(2,1)S(1)} %copy-done.2, f32[512,1536]{1,0:T(8,128)S(1)} %get-tuple-element.10), kind=kOutput, calls=%fused_computation.4 | convolution fusion | flops 4849926144 | bytes 17301504 | tf_op jit(solution)/shard_map/dot_general | solution.py:18
  161.6 0.0 copy-start.1
  161.6 0.0 reduce-scatter.5.cloned.1.call-update
  161.6 0.0 reduce-scatter.7.cloned.1.call-start
  161.6 1.8 copy-done.1
  163.5 13.6 %fusion = bf16[3072,1536]{0,1:T(8,128)(2,1)} fusion(bf16[512,3072]{1,0:T(8,128)(2,1)S(1)} %copy-done.1, bf16[512,1536]{1,0:T(8,128)(2,1)} %param.5, f32[512,1536]{1,0:T(8,128)} %copy-done.3), kind=kOutput, calls=%fused_computation.1 | convolution fusion | flops 4853071872 | bytes 17301504 | tf_op jit(solution)/shard_map/dot_general | solution.py:25
  177.0 12.7 %copy.8 = bf16[3072,1536]{1,0:T(8,128)(2,1)} copy(bf16[3072,1536]{0,1:T(8,128)(2,1)} %fusion) | data formatting | bytes 18874368
  189.7 0.0 reduce-scatter.7.cloned.1.call-update
  189.8 13.5 %reduce-scatter.5.cloned.1.call-done = bf16[512,1536]{1,0:T(8,128)(2,1)} async-done(((bf16[512,3072]{1,0:T(8,128)(2,1)}), bf16[512,1536]{1,0:T(8,128)(2,1)}) %reduce-scatter.5.cloned.1.call-update) | async-done | bytes 1572880 | tf_op jit(solution)/shard_map/reduce_scatter | solution.py:21
  203.2 116.5 %reduce-scatter.7.cloned.1.call-done = bf16[192,1536]{1,0:T(8,128)(2,1)} async-done(((bf16[3072,1536]{1,0:T(8,128)(2,1)}), bf16[192,1536]{1,0:T(8,128)(2,1)}) %reduce-scatter.7.cloned.1.call-update) | async-done | bytes 589840
Async XLA Ops:
  7.2 50.0 %all-gather.3.cloned.1.call-start = ((), (), s32[]{:S(2)}) async-start(), calls=%async_computation.2 | async-start | bytes 4718592 | tf_op jit(solution)/shard_map/all_gather | solution.py:13
  7.9 133.1 %all-gather.5.cloned.1.call-start = ((), (), s32[]{:S(2)}) async-start(), calls=%async_computation.3 | async-start | bytes 10027008 | tf_op jit(solution)/shard_map/all_gather | solution.py:12
  8.6 145.0 %copy-start.2 = (bf16[512,1536]{1,0:T(8,128)(2,1)S(1)}, bf16[512,1536]{1,0:T(8,128)(2,1)}, u32[]{:S(2)}) copy-start(bf16[512,1536]{1,0:T(8,128)(2,1)} %param.5) | copy-start | bytes 4718596
  8.7 194.6 %reduce-scatter.5.cloned.1.call-start = ((), (), s32[]{:S(2)}) async-start(), calls=%async_computation.4 | async-start | bytes 4718592 | tf_op jit(solution)/shard_map/reduce_scatter | solution.py:21
  141.0 12.7 %copy-start = (bf16[3072,1536]{1,0:T(8,128)(2,1)S(1)}, bf16[3072,1536]{1,0:T(8,128)(2,1)}, u32[]{:S(2)}) copy-start(bf16[3072,1536]{1,0:T(8,128)(2,1)} %all-gather.5.cloned.1.call-done) | copy-start | bytes 28311556
  152.0 1.6 copy-start.3
  161.6 1.9 copy-start.1
  161.6 158.1 %reduce-scatter.7.cloned.1.call-start = ((), (), s32[]{:S(2)}) async-start(), calls=%async_computation.5 | async-start | bytes 10027008
Sparse Core Ops, SparseCore 0:
  9.5 47.6 all-gather.2
  59.5 81.4 all-gather.4
  161.7 41.4 reduce-scatter.4
  208.3 111.3 reduce-scatter.6
where the time goes:
time: 327 us; the launch traced here: 326 us
  waiting for transfers between devices  264 us (81%)
  matrix products  32.5 us (10%)
  local copies, waits for them, and re-layouts  16.2 us (5%)
  between operations  13.8 us (4%)
    unnamed x5, waiting for transfers between devices  118 us
    all_gather x1, waiting for transfers between devices, on_device(): weights_all = lax.all_gather(w_in, 'dp', axis=0, tiled=True)  83.8 us
    all_gather x1, waiting for transfers between devices, on_device(): gathered = lax.all_gather(tokens, 'tensor', axis=1, tiled=True)  48.5 us
    unnamed x9, local copies, waits for them, and re-layouts  16.2 us
    dot_general x1, matrix products, on_device(): lax.dot_general(gathered, pre_grad, (((0,), (0,)), ((), ())), preferred_e...  13.6 us
    reduce_scatter x1, waiting for transfers between devices, on_device(): lax.psum_scatter(product.astype(jnp.bfloat16), 'tensor', scatter_dimensio...  13.5 us
    dot_general x1, matrix products, on_device(): preact = jnp.dot(gathered, weights_all, preferred_element_type=jnp.float32)  11 us
    dot_general x1, matrix products, on_device(): lax.dot_general(pre_grad, weights_all, (((1,), (1,)), ((), ())), preferre...  7.93 us
  transfers between devices with their start and end apart: 4, of which 4 were waited for; matrix products, arithmetic and copies ran while one was open for 8% of the time, Pallas kernels for 0%

commit v1 on v0

v1 whole, which is shorter than its diff:
```python
import functools

import jax
import jax.numpy as jnp
from jax import lax
from jax.experimental import pallas as pl
from jax.experimental.pallas import tpu as pltpu
from jax.sharding import PartitionSpec as P

BF16 = jnp.bfloat16
F32 = jnp.float32
GROUPS = 2
DIRS = 2
TILE = 256
RS_LAG = 2
ROOT = 0.7978845608028654


def kernel(
    n, peers, w_hbm, tok_hbm, cot_hbm, hid, xg, wg,
    w_all, tok, tok_t, cot, pg, part, psend, precv, rsend, rrecv, xsend, xrecv,
    load_sem, tok_s, tok_r, ag_s, ag_r, agp_s, agp_r,
    rs_s, rs_r, rsp_s, rsp_r, x_s, x_r,
):
    S = w_hbm.shape[0]
    rows, dx = tok_hbm.shape
    ff = cot_hbm.shape[1]
    gcols = ff // GROUPS
    qcols = gcols // DIRS
    xcols = xsend.shape[2]
    nb = dx // xcols
    halves = rows // TILE
    ntile = gcols // TILE
    units = halves * ntile
    ag_lag = n // 2

    dp = lax.axis_index("dp")
    x = lax.axis_index("tensor")
    c = lax.rem(dp, 2)
    q = lax.div(dp, 2)
    odd = lax.rem(q, 2)
    p = (1 - odd) * lax.div(q, 2) + odd * (n - lax.div(q + 1, 2))

    def chip_at(pos):
        pos = lax.rem(pos + 2 * n, n)
        far = lax.div(pos, n // 2)
        return (1 - far) * 2 * pos + far * (2 * n - 1 - 2 * pos)

    ring_to = [{"dp": chip_at(p + 1) * 2 + c}, {"dp": chip_at(p - 1) * 2 + c}]
    mate = {"dp": q * 2 + 1 - c}

    def peer(t):
        return {"tensor": lax.rem(x + t, peers)}

    w_load = pltpu.make_async_copy(
        w_hbm, w_all.at[pl.ds(pl.multiple_of(dp * S, 16), S), :], load_sem.at[0])
    tok_load = pltpu.make_async_copy(
        tok_hbm, tok.at[:, pl.ds(pl.multiple_of(x * dx, 128), dx)], load_sem.at[1])
    cot_load = pltpu.make_async_copy(cot_hbm, cot, load_sem.at[2])
    w_load.start()
    tok_load.start()
    cot_load.start()

    barrier = pltpu.get_barrier_semaphore()
    for who in ring_to + [mate] + [peer(t) for t in range(1, peers)]:
        pl.semaphore_signal(
            barrier, inc=1, device_id=who, device_id_type=pl.DeviceIdType.MESH)
    pl.semaphore_wait(barrier, 3 + peers - 1)

    def remote(src, dst, ssem, rsem, who):
        return pltpu.make_async_remote_copy(
            src_ref=src, dst_ref=dst, send_sem=ssem, recv_sem=rsem,
            device_id=who, device_id_type=pl.DeviceIdType.MESH)

    def w_piece(g, d, pos):
        owner = chip_at(pos) * 2 + c
        return w_all.at[pl.ds(pl.multiple_of(owner * S, 16), S),
                        pl.ds(g * gcols + d * qcols, qcols)]

    def w_piece_mate(g, d, pos):
        owner = chip_at(pos) * 2 + 1 - c
        return w_all.at[pl.ds(pl.multiple_of(owner * S, 16), S),
                        pl.ds(g * gcols + d * qcols, qcols)]

    def sign(d):
        return 1 - 2 * d

    def ag_ring(g, d, h):
        piece = w_piece(g, d, p - sign(d) * h)
        k = (g * DIRS + d) * n + h
        return remote(piece, piece, ag_s.at[k], ag_r.at[k], ring_to[d])

    def ag_ring_in(g, d, h):
        piece = w_piece(g, d, p - sign(d) * (h + 1))
        k = (g * DIRS + d) * n + h
        return remote(piece, piece, ag_s.at[k], ag_r.at[k], ring_to[d])

    def ag_mate(g, d, h):
        piece = w_piece(g, d, p - sign(d) * h)
        k = (g * DIRS + d) * n + h
        return remote(piece, piece, agp_s.at[k], agp_r.at[k], mate)

    def ag_mate_in(g, d, h):
        piece = w_piece_mate(g, d, p - sign(d) * h)
        k = (g * DIRS + d) * n + h
        return remote(piece, piece, agp_s.at[k], agp_r.at[k], mate)

    def tok_copy(t, m):
        piece = tok.at[pl.ds(m * TILE, TILE), pl.ds(pl.multiple_of(x * dx, 128), dx)]
        k = (t - 1) * halves + m
        return remote(piece, piece, tok_s.at[k], tok_r.at[k], peer(t))

    def tok_in(t, m):
        source = lax.rem(x + peers - t, peers)
        piece = tok.at[pl.ds(m * TILE, TILE), pl.ds(pl.multiple_of(source * dx, 128), dx)]
        k = (t - 1) * halves + m
        return remote(piece, piece, tok_s.at[k], tok_r.at[k], peer(t))

    def ag_start(g):
        for d in range(DIRS):
            ag_ring(g, d, 0).start()
        for d in range(DIRS):
            ag_mate(g, d, 0).start()

    w_load.wait()
    ag_start(0)
    tok_load.wait()
    for m in range(halves):
        for t in range(1, peers):
            tok_copy(t, m).start()
    cot_load.wait()

    def wait_mates(g):
        @pl.loop(0, n)
        def _(h):
            for d in range(DIRS):
                ag_mate_in(g, d, h).wait_recv()

    def activate(g, u):
        m = lax.div(u, ntile)
        rsl = pl.ds(pl.multiple_of(m * TILE, TILE), TILE)
        csl = pl.ds(pl.multiple_of(g * gcols + lax.rem(u, ntile) * TILE, TILE), TILE)
        v = jnp.dot(tok[rsl, :], w_all[:, csl], preferred_element_type=F32)
        sq = v * v
        th = jnp.tanh(ROOT * v * (1.0 + 0.044715 * sq))
        half = 0.5 * (1.0 + th)
        hid[rsl, csl] = (v * half).astype(BF16)
        slope = half + 0.5 * v * (1.0 - th * th) * (ROOT * (1.0 + 3.0 * 0.044715 * sq))
        pg[rsl, csl] = (cot[rsl, csl].astype(F32) * slope).astype(BF16)

    @pl.loop(0, n - 1 + ag_lag)
    def _(s):
        for g in range(GROUPS):
            h = s - g * ag_lag

            @pl.when((h >= 0) & (h < n - 1))
            def _():
                for d in range(DIRS):
                    ag_ring_in(g, d, h).wait_recv()

                    @pl.when(h < n - 2)
                    def _():
                        ag_ring(g, d, h + 1).start()

                    ag_mate(g, d, h + 1).start()

        @pl.when(s == ag_lag - 1)
        def _():
            ag_start(1)

        @pl.when(s == n - 1)
        def _():
            wait_mates(0)

        late = s - (n - 1)

        @pl.when(late >= 0)
        def _():
            @pl.loop(lax.div(late * units, ag_lag), lax.div((late + 1) * units, ag_lag))
            def _(u):
                for m in range(halves):
                    @pl.when(u == m * ntile)
                    def _():
                        for t in range(1, peers):
                            tok_in(t, m).wait_recv()

                        @pl.loop(0, tok.shape[1] // TILE)
                        def _(k):
                            at = pl.ds(pl.multiple_of(k * TILE, TILE), TILE)
                            tok_t[at, m * TILE:(m + 1) * TILE] = (
                                tok[m * TILE:(m + 1) * TILE, at].T)

                activate(0, u)

    def rs_owner(d, h):
        return chip_at(p - sign(d) * (h + 1))

    def slot(g, d, h):
        return (g * DIRS + d) * n + h

    def rs_ring(g, d, h):
        k = slot(g, d, h)
        return remote(rsend.at[k], rrecv.at[k], rs_s.at[k], rs_r.at[k], ring_to[d])

    def rs_mate(g, d, h):
        k = slot(g, d, h)
        return remote(psend.at[k], precv.at[k], rsp_s.at[k], rsp_r.at[k], mate)

    def make_part(g, d, h):
        cols = g * gcols + d * qcols
        acc = part.at[g * DIRS + d]
        acc[...] = jnp.dot(
            tok_t[pl.ds(pl.multiple_of(rs_owner(d, h) * 2 * S, 16), 2 * S), :],
            pg[:, cols:cols + qcols], preferred_element_type=F32)
        psend[slot(g, d, h)] = acc[pl.ds(pl.multiple_of((1 - c) * S, 16), S), :].astype(BF16)
        rs_mate(g, d, h).start()

    def combine(g, d, h):
        k = slot(g, d, h)
        cols = g * gcols + d * qcols
        acc = part.at[g * DIRS + d]
        mine = pl.ds(pl.multiple_of(c * S, 16), S)
        rs_mate(g, d, h).wait_recv()

        @pl.when(h == 0)
        def _():
            rsend[k] = (acc[mine, :] + precv[k].astype(F32)).astype(BF16)

        @pl.when(h > 0)
        def _():
            rs_ring(g, d, h - 1).wait_recv()
            total = (acc[mine, :] + precv[k].astype(F32)
                     + rrecv[k - 1].astype(F32)).astype(BF16)

            @pl.when(h < n - 1)
            def _():
                rsend[k] = total

            @pl.when(h == n - 1)
            def _():
                wg[:, cols:cols + qcols] = total

        @pl.when(h < n - 1)
        def _():
            rs_ring(g, d, h).start()

    def x_block(owner, b):
        at = pl.ds(pl.multiple_of(owner * dx + b * xcols, 128), xcols)
        return lax.dot_general(
            pg[...], w_all[at, :], (((1,), (1,)), ((), ())),
            preferred_element_type=F32).astype(BF16)

    def x_copy(k):
        return remote(xsend.at[k], xrecv.at[k], x_s.at[k], x_r.at[k],
                      peer(lax.div(k, nb) + 1))

    away = (peers - 1) * nb

    @pl.loop(-1, n + RS_LAG)
    def _(s):
        for g in range(GROUPS):
            h = s - g * RS_LAG

            @pl.when((h >= 0) & (h < n))
            def _():
                for d in range(DIRS):
                    combine(g, d, h)

            if g == 1:
                @pl.when((s >= 0) & (s < RS_LAG))
                def _():
                    @pl.when(s == 0)
                    def _():
                        wait_mates(1)

                    @pl.loop(lax.div(s * units, RS_LAG), lax.div((s + 1) * units, RS_LAG))
                    def _(u):
                        activate(1, u)

            @pl.when((h >= -1) & (h < n - 1))
            def _():
                for d in range(DIRS):
                    make_part(g, d, h + 1)

        e = s - RS_LAG

        @pl.when((e >= 0) & (e < 2))
        def _():
            @pl.loop(lax.div(e * away, 2), lax.div((e + 1) * away, 2))
            def _(k):
                t = lax.div(k, nb) + 1
                xsend[k] = x_block(lax.rem(x + t, peers), lax.rem(k, nb))
                x_copy(k).start()

        @pl.when((e >= 2) & (e < 4))
        def _():
            @pl.loop(lax.div((e - 2) * nb, 2), lax.div((e - 1) * nb, 2))
            def _(b):
                xg[:, pl.ds(pl.multiple_of(b * xcols, 128), xcols)] = x_block(x, b)

    @pl.loop(0, nb)
    def _(b):
        at = pl.ds(pl.multiple_of(b * xcols, 128), xcols)
        total = xg[:, at].astype(F32)
        for t in range(1, peers):
            k = (t - 1) * nb + b
            x_copy(k).wait_recv()
            total = total + xrecv[k].astype(F32)
        xg[:, at] = total.astype(BF16)

    @pl.loop(0, n)
    def _(h):
        for g in range(GROUPS):
            for d in range(DIRS):
                ag_mate(g, d, h).wait_send()
                rs_mate(g, d, h).wait_send()

                @pl.when(h < n - 1)
                def _():
                    ag_ring(g, d, h).wait_send()
                    rs_ring(g, d, h).wait_send()

    @pl.loop(0, away)
    def _(k):
        x_copy(k).wait_send()

    for m in range(halves):
        for t in range(1, peers):
            tok_copy(t, m).wait_send()


def on_device(n_dp, peers, tokens, w_in, cotangent):
    n = n_dp // 2
    S, ff = w_in.shape
    rows, dx = tokens.shape
    D = dx * peers
    qcols = ff // (GROUPS * DIRS)
    xcols = min(384, dx)
    nx = (peers - 1) * (dx // xcols)
    slots = GROUPS * DIRS * n
    any_spec = pl.BlockSpec(memory_space=pl.ANY)
    vmem = pl.BlockSpec(memory_space=pltpu.VMEM)
    dma = pltpu.SemaphoreType.DMA
    halves = rows // TILE
    return pl.pallas_call(
        functools.partial(kernel, n, peers),
        out_shape=[
            jax.ShapeDtypeStruct((rows, ff), BF16),
            jax.ShapeDtypeStruct((rows, dx), BF16),
            jax.ShapeDtypeStruct((S, ff), BF16),
        ],
        in_specs=[any_spec] * 3,
        out_specs=[vmem] * 3,
        scratch_shapes=[
            pltpu.VMEM((D, ff), BF16),
            pltpu.VMEM((rows, D), BF16),
            pltpu.VMEM((D, rows), BF16),
            pltpu.VMEM((rows, ff), BF16),
            pltpu.VMEM((rows, ff), BF16),
            pltpu.VMEM((GROUPS * DIRS, 2 * S, qcols), F32),
            pltpu.VMEM((slots, S, qcols), BF16),
            pltpu.VMEM((slots, S, qcols), BF16),
            pltpu.VMEM((slots, S, qcols), BF16),
            pltpu.VMEM((slots, S, qcols), BF16),
            pltpu.VMEM((nx, rows, xcols), BF16),
            pltpu.VMEM((nx, rows, xcols), BF16),
            dma((3,)),
            dma(((peers - 1) * halves,)), dma(((peers - 1) * halves,)),
            dma((slots,)), dma((slots,)), dma((slots,)), dma((slots,)),
            dma((slots,)), dma((slots,)), dma((slots,)), dma((slots,)),
            dma((nx,)), dma((nx,)),
        ],
        compiler_params=pltpu.CompilerParams(
            collective_id=0, has_side_effects=True,
            vmem_limit_bytes=60 * 1024 * 1024,
        ),
        cost_estimate=pl.CostEstimate(
            flops=6 * rows * D * ff, bytes_accessed=4 * (2 * rows * ff + rows * dx + S * ff),
            transcendentals=rows * ff),
    )(w_in, tokens, cotangent)


def solution(mesh):
    spec = P("dp", "tensor")
    return jax.shard_map(
        functools.partial(on_device, mesh.shape["dp"], mesh.shape["tensor"]),
        mesh=mesh, in_specs=(spec,) * 3, out_specs=(spec,) * 3, check_vma=False,
    )
```

time: 327 us -> 128 us (0.39)
  waiting for transfers between devices: 264 us -> 0 us
  Pallas kernels: 0 us -> 122 us
  matrix products: 32.5 us -> 0 us
  between operations: 13.8 us -> 0.65 us
  local copies, waits for them, and re-layouts: 16.2 us -> 5.05 us
    all_gather x2 -> x0, waiting for transfers between devices: 132 us -> none  [the longest x1 83.8 us: on_device(): weights_all = lax.all_gather(w_in, 'dp', axis=0, tiled=True)]
    pallas_call x0 -> x1, Pallas kernels: none -> 122 us  [on_device(): pl.pallas_call(functools.partial(kernel, n, peers), out_shape=[jax.ShapeD...]
    unnamed x5 -> x0, waiting for transfers between devices: 118 us -> none
    dot_general x3 -> x0, matrix products: 32.5 us -> none  [the longest x1 13.6 us: on_device(): lax.dot_general(gathered, pre_grad, (((0,), (0,)), ((), ())), preferred_e...]
    reduce_scatter x1 -> x0, waiting for transfers between devices: 13.5 us -> none  [on_device(): lax.psum_scatter(product.astype(jnp.bfloat16), 'tensor', scatter_dimensio...]
    unnamed x9 -> x7, local copies, waits for them, and re-layouts: 16.2 us -> 5.05 us
  transfers between devices with their start and end apart: 4 -> 0, of which waited for: 4 -> 0; matrix products, arithmetic and copies ran while one was open for 8% -> 0% of each run, Pallas kernels for 0% -> 0%
where the time goes in v1:
time: 128 us; the launch traced here: 127 us
  Pallas kernels  122 us (95%)
  local copies, waits for them, and re-layouts  5.05 us (4%)
    pallas_call x1, Pallas kernels, on_device(): pl.pallas_call(functools.partial(kernel, n, peers), out_shape=[jax.ShapeD...  122 us
    unnamed x7, local copies, waits for them, and re-layouts  5.05 us

profile of v1, /device:TPU:0, one launch (start us, length us, event | category | flops | bytes accessed | tf_op | source)
XLA Modules:
  0.0 127.3 jit_solution(16491571561835706882)
XLA Ops:
  0.6 121.6 %shard_map.58 = (bf16[512,1536]{1,0:T(8,128)(2,1)}, bf16[512,1536]{1,0:T(8,128)(2,1)}, bf16[192,1536]{1,0:T(8,128)(2,1)}) custom-call(bf16[192,1536]{1,0:T(8,128)(2,1)} %w_hbm.1, bf16[512,1536]{1,0:T(8,128)(2,1)} %tok_hbm.1, bf16[512,1536]{1,0:T(8,128)(2,1)} %cot_hbm.1), custom_call_target="tpu_custom_call" | custom-call | flops 14495514624 | bytes 10616832 | tf_op jit(solution)/shard_map/pallas_call | solution.py:345
  122.3 0.0 copy-start
  122.3 2.8 %copy.9 = bf16[512,1536]{1,0:T(8,128)(2,1)} copy(bf16[512,1536]{1,0:T(8,128)(2,1)} %get-tuple-element.6) | data formatting | bytes 3145728
  125.0 0.0 copy-done
  125.0 0.0 copy-start.1
  125.0 1.1 copy.10
  126.2 0.3 copy-done.1
  126.5 0.8 copy.11
Async XLA Ops:
  122.3 2.8 %copy-start = (bf16[512,1536]{1,0:T(8,128)(2,1)S(1)}, bf16[512,1536]{1,0:T(8,128)(2,1)}, u32[]{:S(2)}) copy-start(bf16[512,1536]{1,0:T(8,128)(2,1)} %get-tuple-element.7) | copy-start | bytes 4718596
  125.0 1.5 %copy-start.1 = (bf16[192,1536]{1,0:T(8,128)(2,1)S(1)}, bf16[192,1536]{1,0:T(8,128)(2,1)}, u32[]{:S(2)}) copy-start(bf16[192,1536]{1,0:T(8,128)(2,1)} %get-tuple-element.8) | copy-start | bytes 1769476

commit v2 on v1

--- a/solution.py
+++ b/solution.py
@@ -12,7 +12,8 @@
 GROUPS = 2
 DIRS = 2
 TILE = 256
-RS_LAG = 2
+SPLIT = 2
+RS_LAG = 4
 ROOT = 0.7978845608028654
 
 
@@ -33,6 +34,7 @@
     ntile = gcols // TILE
     units = halves * ntile
     ag_lag = n // 2
+    sr = S // SPLIT
 
     dp = lax.axis_index("dp")
     x = lax.axis_index("tensor")
@@ -72,37 +74,25 @@
             src_ref=src, dst_ref=dst, send_sem=ssem, recv_sem=rsem,
             device_id=who, device_id_type=pl.DeviceIdType.MESH)
 
-    def w_piece(g, d, pos):
-        owner = chip_at(pos) * 2 + c
-        return w_all.at[pl.ds(pl.multiple_of(owner * S, 16), S),
+    def w_piece(g, d, pos, core, r):
+        owner = chip_at(pos) * 2 + core
+        return w_all.at[pl.ds(pl.multiple_of(owner * S + r * sr, 16), sr),
                         pl.ds(g * gcols + d * qcols, qcols)]
 
-    def w_piece_mate(g, d, pos):
-        owner = chip_at(pos) * 2 + 1 - c
-        return w_all.at[pl.ds(pl.multiple_of(owner * S, 16), S),
-                        pl.ds(g * gcols + d * qcols, qcols)]
+    def sem_at(g, d, h, r):
+        return ((g * DIRS + d) * SPLIT + r) * n + h
 
     def sign(d):
         return 1 - 2 * d
 
-    def ag_ring(g, d, h):
-        piece = w_piece(g, d, p - sign(d) * h)
-        k = (g * DIRS + d) * n + h
+    def ag_ring(g, d, h, r, back=0):
+        piece = w_piece(g, d, p - sign(d) * (h + back), c, r)
+        k = sem_at(g, d, h, r)
         return remote(piece, piece, ag_s.at[k], ag_r.at[k], ring_to[d])
 
-    def ag_ring_in(g, d, h):
-        piece = w_piece(g, d, p - sign(d) * (h + 1))
-        k = (g * DIRS + d) * n + h
-        return remote(piece, piece, ag_s.at[k], ag_r.at[k], ring_to[d])
-
-    def ag_mate(g, d, h):
-        piece = w_piece(g, d, p - sign(d) * h)
-        k = (g * DIRS + d) * n + h
-        return remote(piece, piece, agp_s.at[k], agp_r.at[k], mate)
-
-    def ag_mate_in(g, d, h):
-        piece = w_piece_mate(g, d, p - sign(d) * h)
-        k = (g * DIRS + d) * n + h
+    def ag_mate(g, d, h, r, core):
+        piece = w_piece(g, d, p - sign(d) * h, core, r)
+        k = sem_at(g, d, h, r)
         return remote(piece, piece, agp_s.at[k], agp_r.at[k], mate)
 
     def tok_copy(t, m):
@@ -117,10 +107,12 @@
         return remote(piece, piece, tok_s.at[k], tok_r.at[k], peer(t))
 
     def ag_start(g):
-        for d in range(DIRS):
-            ag_ring(g, d, 0).start()
-        for d in range(DIRS):
-            ag_mate(g, d, 0).start()
+        for r in range(SPLIT):
+            for d in range(DIRS):
+                ag_ring(g, d, 0, r).start()
+        for r in range(SPLIT):
+            for d in range(DIRS):
+                ag_mate(g, d, 0, r, c).start()
 
     w_load.wait()
     ag_start(0)
@@ -133,8 +125,9 @@
     def wait_mates(g):
         @pl.loop(0, n)
         def _(h):
-            for d in range(DIRS):
-                ag_mate_in(g, d, h).wait_recv()
+            for r in range(SPLIT):
+                for d in range(DIRS):
+                    ag_mate(g, d, h, r, 1 - c).wait_recv()
 
     def activate(g, u):
         m = lax.div(u, ntile)
@@ -148,59 +141,17 @@
         slope = half + 0.5 * v * (1.0 - th * th) * (ROOT * (1.0 + 3.0 * 0.044715 * sq))
         pg[rsl, csl] = (cot[rsl, csl].astype(F32) * slope).astype(BF16)
 
-    @pl.loop(0, n - 1 + ag_lag)
-    def _(s):
-        for g in range(GROUPS):
-            h = s - g * ag_lag
-
-            @pl.when((h >= 0) & (h < n - 1))
-            def _():
-                for d in range(DIRS):
-                    ag_ring_in(g, d, h).wait_recv()
-
-                    @pl.when(h < n - 2)
-                    def _():
-                        ag_ring(g, d, h + 1).start()
-
-                    ag_mate(g, d, h + 1).start()
-
-        @pl.when(s == ag_lag - 1)
-        def _():
-            ag_start(1)
-
-        @pl.when(s == n - 1)
-        def _():
-            wait_mates(0)
-
-        late = s - (n - 1)
-
-        @pl.when(late >= 0)
-        def _():
-            @pl.loop(lax.div(late * units, ag_lag), lax.div((late + 1) * units, ag_lag))
-            def _(u):
-                for m in range(halves):
-                    @pl.when(u == m * ntile)
-                    def _():
-                        for t in range(1, peers):
-                            tok_in(t, m).wait_recv()
-
-                        @pl.loop(0, tok.shape[1] // TILE)
-                        def _(k):
-                            at = pl.ds(pl.multiple_of(k * TILE, TILE), TILE)
-                            tok_t[at, m * TILE:(m + 1) * TILE] = (
-                                tok[m * TILE:(m + 1) * TILE, at].T)
-
-                activate(0, u)
-
     def rs_owner(d, h):
         return chip_at(p - sign(d) * (h + 1))
 
     def slot(g, d, h):
         return (g * DIRS + d) * n + h
 
-    def rs_ring(g, d, h):
+    def rs_ring(g, d, h, r):
         k = slot(g, d, h)
-        return remote(rsend.at[k], rrecv.at[k], rs_s.at[k], rs_r.at[k], ring_to[d])
+        at = pl.ds(r * sr, sr)
+        j = sem_at(g, d, h, r)
+        return remote(rsend.at[k, at], rrecv.at[k, at], rs_s.at[j], rs_r.at[j], ring_to[d])
 
     def rs_mate(g, d, h):
         k = slot(g, d, h)
@@ -215,34 +166,94 @@
         psend[slot(g, d, h)] = acc[pl.ds(pl.multiple_of((1 - c) * S, 16), S), :].astype(BF16)
         rs_mate(g, d, h).start()
 
-    def combine(g, d, h):
+    def combine(g, h):
+        for d in range(DIRS):
+            rs_mate(g, d, h).wait_recv()
+        for r in range(SPLIT):
+            for d in range(DIRS):
+                combine_piece(g, d, h, r)
+
+    def combine_piece(g, d, h, r):
         k = slot(g, d, h)
+        at = pl.ds(r * sr, sr)
         cols = g * gcols + d * qcols
-        acc = part.at[g * DIRS + d]
-        mine = pl.ds(pl.multiple_of(c * S, 16), S)
-        rs_mate(g, d, h).wait_recv()
+        mine = part[g * DIRS + d, pl.ds(pl.multiple_of(c * S + r * sr, 16), sr), :]
+        total = mine + precv[k, at].astype(F32)
 
         @pl.when(h == 0)
         def _():
-            rsend[k] = (acc[mine, :] + precv[k].astype(F32)).astype(BF16)
+            rsend[k, at] = total.astype(BF16)
 
         @pl.when(h > 0)
         def _():
-            rs_ring(g, d, h - 1).wait_recv()
-            total = (acc[mine, :] + precv[k].astype(F32)
-                     + rrecv[k - 1].astype(F32)).astype(BF16)
+            rs_ring(g, d, h - 1, r).wait_recv()
+            full = (total + rrecv[k - 1, at].astype(F32)).astype(BF16)
 
             @pl.when(h < n - 1)
             def _():
-                rsend[k] = total
+                rsend[k, at] = full
 
             @pl.when(h == n - 1)
             def _():
-                wg[:, cols:cols + qcols] = total
+                wg[at, cols:cols + qcols] = full
 
         @pl.when(h < n - 1)
         def _():
-            rs_ring(g, d, h).start()
+            rs_ring(g, d, h, r).start()
+
+    @pl.loop(0, n - 1 + ag_lag)
+    def _(s):
+        late = s - (n - 1)
+
+        @pl.when(late == ag_lag - 1)
+        def _():
+            for d in range(DIRS):
+                make_part(0, d, 0)
+            combine(0, 0)
+            for d in range(DIRS):
+                make_part(0, d, 1)
+
+        for g in range(GROUPS):
+            h = s - g * ag_lag
+
+            @pl.when((h >= 0) & (h < n - 1))
+            def _():
+                for r in range(SPLIT):
+                    for d in range(DIRS):
+                        ag_ring(g, d, h, r, 1).wait_recv()
+
+                        @pl.when(h < n - 2)
+                        def _():
+                            ag_ring(g, d, h + 1, r).start()
+
+                        ag_mate(g, d, h + 1, r, c).start()
+
+        @pl.when(s == ag_lag - 1)
+        def _():
+            ag_start(1)
+
+        @pl.when(s == n - 1)
+        def _():
+            wait_mates(0)
+
+        @pl.when((late >= 0) & (late < ag_lag - 1))
+        def _():
+            @pl.loop(lax.div(late * units, ag_lag - 1),
+                     lax.div((late + 1) * units, ag_lag - 1))
+            def _(u):
+                for m in range(halves):
+                    @pl.when(u == m * ntile)
+                    def _():
+                        for t in range(1, peers):
+                            tok_in(t, m).wait_recv()
+
+                        @pl.loop(0, tok.shape[1] // TILE)
+                        def _(k):
+                            at = pl.ds(pl.multiple_of(k * TILE, TILE), TILE)
+                            tok_t[at, m * TILE:(m + 1) * TILE] = (
+                                tok[m * TILE:(m + 1) * TILE, at].T)
+
+                activate(0, u)
 
     def x_block(owner, b):
         at = pl.ds(pl.multiple_of(owner * dx + b * xcols, 128), xcols)
@@ -256,24 +267,24 @@
 
     away = (peers - 1) * nb
 
-    @pl.loop(-1, n + RS_LAG)
+    @pl.loop(1, n + RS_LAG)
     def _(s):
         for g in range(GROUPS):
             h = s - g * RS_LAG
 
             @pl.when((h >= 0) & (h < n))
             def _():
-                for d in range(DIRS):
-                    combine(g, d, h)
+                combine(g, h)
 
             if g == 1:
-                @pl.when((s >= 0) & (s < RS_LAG))
+                @pl.when(s < RS_LAG)
                 def _():
-                    @pl.when(s == 0)
+                    @pl.when(s == 1)
                     def _():
                         wait_mates(1)
 
-                    @pl.loop(lax.div(s * units, RS_LAG), lax.div((s + 1) * units, RS_LAG))
+                    @pl.loop(lax.div((s - 1) * units, RS_LAG - 1),
+                             lax.div(s * units, RS_LAG - 1))
                     def _(u):
                         activate(1, u)
 
@@ -312,13 +323,14 @@
     def _(h):
         for g in range(GROUPS):
             for d in range(DIRS):
-                ag_mate(g, d, h).wait_send()
                 rs_mate(g, d, h).wait_send()
-
-                @pl.when(h < n - 1)
-                def _():
-                    ag_ring(g, d, h).wait_send()
-                    rs_ring(g, d, h).wait_send()
+                for r in range(SPLIT):
+                    ag_mate(g, d, h, r, c).wait_send()
+
+                    @pl.when(h < n - 1)
+                    def _():
+                        ag_ring(g, d, h, r).wait_send()
+                        rs_ring(g, d, h, r).wait_send()
 
     @pl.loop(0, away)
     def _(k):
@@ -366,8 +378,9 @@
             pltpu.VMEM((nx, rows, xcols), BF16),
             dma((3,)),
             dma(((peers - 1) * halves,)), dma(((peers - 1) * halves,)),
-            dma((slots,)), dma((slots,)), dma((slots,)), dma((slots,)),
-            dma((slots,)), dma((slots,)), dma((slots,)), dma((slots,)),
+            dma((slots * SPLIT,)), dma((slots * SPLIT,)),
+            dma((slots * SPLIT,)), dma((slots * SPLIT,)),
+            dma((slots * SPLIT,)), dma((slots * SPLIT,)), dma((slots,)), dma((slots,)),
             dma((nx,)), dma((nx,)),
         ],
         compiler_params=pltpu.CompilerParams(

time: 128 us -> 123 us (0.961)
  Pallas kernels: 122 us -> 118 us
    pallas_call x1, Pallas kernels: 122 us -> 118 us  [on_device(): pl.pallas_call(functools.partial(kernel, n, peers), out_shape=[jax.ShapeD...]
where the time goes in v2:
time: 123 us
  Pallas kernels  118 us (96%)
  local copies, waits for them, and re-layouts  5.05 us (4%)
    pallas_call x1, Pallas kernels, on_device(): pl.pallas_call(functools.partial(kernel, n, peers), out_shape=[jax.ShapeD...  118 us
    unnamed x7, local copies, waits for them, and re-layouts  5.05 us

profile of v2, /device:TPU:0, one launch (start us, length us, event | category | flops | bytes accessed | tf_op | source)
XLA Modules:
  0.0 123.3 jit_solution(12843452646258748886)
XLA Ops:
  0.6 117.6 %shard_map.58 = (bf16[512,1536]{1,0:T(8,128)(2,1)}, bf16[512,1536]{1,0:T(8,128)(2,1)}, bf16[192,1536]{1,0:T(8,128)(2,1)}) custom-call(bf16[192,1536]{1,0:T(8,128)(2,1)} %w_hbm.1, bf16[512,1536]{1,0:T(8,128)(2,1)} %tok_hbm.1, bf16[512,1536]{1,0:T(8,128)(2,1)} %cot_hbm.1), custom_call_target="tpu_custom_call" | custom-call | flops 14495514624 | bytes 10616832 | tf_op jit(solution)/shard_map/pallas_call | solution.py:357
  118.2 0.0 copy-start
  118.2 2.8 %copy.9 = bf16[512,1536]{1,0:T(8,128)(2,1)} copy(bf16[512,1536]{1,0:T(8,128)(2,1)} %get-tuple-element.6) | data formatting | bytes 3145728
  121.0 0.0 copy-done
  121.0 0.0 copy-start.1
  121.0 1.1 copy.10
  122.1 0.3 copy-done.1
  122.5 0.8 copy.11
Async XLA Ops:
  118.2 2.8 %copy-start = (bf16[512,1536]{1,0:T(8,128)(2,1)S(1)}, bf16[512,1536]{1,0:T(8,128)(2,1)}, u32[]{:S(2)}) copy-start(bf16[512,1536]{1,0:T(8,128)(2,1)} %get-tuple-element.7) | copy-start | bytes 4718596
  121.0 1.5 %copy-start.1 = (bf16[192,1536]{1,0:T(8,128)(2,1)S(1)}, bf16[192,1536]{1,0:T(8,128)(2,1)}, u32[]{:S(2)}) copy-start(bf16[192,1536]{1,0:T(8,128)(2,1)} %get-tuple-element.8) | copy-start | bytes 1769476

commit v3 on v2

--- a/solution.py
+++ b/solution.py
@@ -9,11 +9,11 @@
 
 BF16 = jnp.bfloat16
 F32 = jnp.float32
-GROUPS = 2
+GROUPS = 3
 DIRS = 2
 TILE = 256
 SPLIT = 2
-RS_LAG = 4
+RS_LAG = 3
 ROOT = 0.7978845608028654
 
 
@@ -33,7 +33,8 @@
     halves = rows // TILE
     ntile = gcols // TILE
     units = halves * ntile
-    ag_lag = n // 2
+    ag_lag = max(2, 3 * n // 8)
+    last = 2 * ag_lag - 1
     sr = S // SPLIT
 
     dp = lax.axis_index("dp")
@@ -201,11 +202,29 @@
         def _():
             rs_ring(g, d, h, r).start()
 
-    @pl.loop(0, n - 1 + ag_lag)
+    strips = dx // 128
+    others = (peers - 1) * strips
+
+    def spread(count, i, steps):
+        return lax.div(i * count, steps), lax.div((i + 1) * count, steps)
+
+    def flip(m, col):
+        at = pl.ds(pl.multiple_of(col, 128), 128)
+        tok_t[at, m * TILE:(m + 1) * TILE] = tok[m * TILE:(m + 1) * TILE, at].T
+
+    def flip_other(m, k):
+        t = lax.div(k, strips) + 1
+        flip(m, lax.rem(x + t, peers) * dx + lax.rem(k, strips) * 128)
+
+    def await_tokens(m):
+        for t in range(1, peers):
+            tok_in(t, m).wait_recv()
+
+    @pl.loop(0, n - 1 + 2 * ag_lag)
     def _(s):
         late = s - (n - 1)
 
-        @pl.when(late == ag_lag - 1)
+        @pl.when(late == last)
         def _():
             for d in range(DIRS):
                 make_part(0, d, 0)
@@ -228,32 +247,50 @@
 
                         ag_mate(g, d, h + 1, r, c).start()
 
-        @pl.when(s == ag_lag - 1)
-        def _():
-            ag_start(1)
-
-        @pl.when(s == n - 1)
+            if g + 1 < GROUPS:
+                @pl.when(h == ag_lag - 1)
+                def _():
+                    ag_start(g + 1)
+
+        @pl.when(late < 0)
+        def _():
+            @pl.loop(*spread(strips, s, n - 1))
+            def _(k):
+                for m in range(halves):
+                    flip(m, x * dx + k * 128)
+
+        @pl.when(late == 0)
         def _():
             wait_mates(0)
-
-        @pl.when((late >= 0) & (late < ag_lag - 1))
-        def _():
-            @pl.loop(lax.div(late * units, ag_lag - 1),
-                     lax.div((late + 1) * units, ag_lag - 1))
+            await_tokens(0)
+
+        @pl.when((late >= 0) & (late < ag_lag))
+        def _():
+            @pl.loop(*spread(units, late, ag_lag))
             def _(u):
-                for m in range(halves):
-                    @pl.when(u == m * ntile)
-                    def _():
-                        for t in range(1, peers):
-                            tok_in(t, m).wait_recv()
-
-                        @pl.loop(0, tok.shape[1] // TILE)
-                        def _(k):
-                            at = pl.ds(pl.multiple_of(k * TILE, TILE), TILE)
-                            tok_t[at, m * TILE:(m + 1) * TILE] = (
-                                tok[m * TILE:(m + 1) * TILE, at].T)
+                @pl.when(u == ntile)
+                def _():
+                    await_tokens(1)
 
                 activate(0, u)
+
+            @pl.loop(*spread(others, late, ag_lag))
+            def _(k):
+                flip_other(0, k)
+
+        @pl.when(late == ag_lag)
+        def _():
+            wait_mates(1)
+
+        @pl.when((late >= ag_lag) & (late < last))
+        def _():
+            @pl.loop(*spread(others, late - ag_lag, ag_lag - 1))
+            def _(k):
+                flip_other(1, k)
+
+            @pl.loop(*spread(units, late - ag_lag, ag_lag - 1))
+            def _(u):
+                activate(1, u)
 
     def x_block(owner, b):
         at = pl.ds(pl.multiple_of(owner * dx + b * xcols, 128), xcols)
@@ -267,45 +304,43 @@
 
     away = (peers - 1) * nb
 
-    @pl.loop(1, n + RS_LAG)
+    @pl.loop(1, n + 2 * RS_LAG)
     def _(s):
+        @pl.when(s == 1)
+        def _():
+            wait_mates(2)
+
         for g in range(GROUPS):
             h = s - g * RS_LAG
 
             @pl.when((h >= 0) & (h < n))
             def _():
                 combine(g, h)
-
-            if g == 1:
-                @pl.when(s < RS_LAG)
-                def _():
-                    @pl.when(s == 1)
-                    def _():
-                        wait_mates(1)
-
-                    @pl.loop(lax.div((s - 1) * units, RS_LAG - 1),
-                             lax.div(s * units, RS_LAG - 1))
-                    def _(u):
-                        activate(1, u)
 
             @pl.when((h >= -1) & (h < n - 1))
             def _():
                 for d in range(DIRS):
                     make_part(g, d, h + 1)
 
-        e = s - RS_LAG
+        @pl.when(s < 3)
+        def _():
+            @pl.loop(*spread(units, s - 1, 2))
+            def _(u):
+                activate(2, u)
+
+        e = s - 3
 
         @pl.when((e >= 0) & (e < 2))
         def _():
-            @pl.loop(lax.div(e * away, 2), lax.div((e + 1) * away, 2))
+            @pl.loop(*spread(away, e, 2))
             def _(k):
                 t = lax.div(k, nb) + 1
                 xsend[k] = x_block(lax.rem(x + t, peers), lax.rem(k, nb))
                 x_copy(k).start()
 
-        @pl.when((e >= 2) & (e < 4))
-        def _():
-            @pl.loop(lax.div((e - 2) * nb, 2), lax.div((e - 1) * nb, 2))
+        @pl.when((e >= 2) & (e < 6))
+        def _():
+            @pl.loop(*spread(nb, e - 2, 4))
             def _(b):
                 xg[:, pl.ds(pl.multiple_of(b * xcols, 128), xcols)] = x_block(x, b)
 
@@ -350,16 +385,16 @@
     xcols = min(384, dx)
     nx = (peers - 1) * (dx // xcols)
     slots = GROUPS * DIRS * n
-    any_spec = pl.BlockSpec(memory_space=pl.ANY)
+    any_spec = pl.BlockSpec(memory_space=pltpu.HBM)
     vmem = pl.BlockSpec(memory_space=pltpu.VMEM)
     dma = pltpu.SemaphoreType.DMA
     halves = rows // TILE
     return pl.pallas_call(
         functools.partial(kernel, n, peers),
         out_shape=[
-            jax.ShapeDtypeStruct((rows, ff), BF16),
-            jax.ShapeDtypeStruct((rows, dx), BF16),
-            jax.ShapeDtypeStruct((S, ff), BF16),
+            pltpu.VMEM((rows, ff), BF16),
+            pltpu.VMEM((rows, dx), BF16),
+            pltpu.VMEM((S, ff), BF16),
         ],
         in_specs=[any_spec] * 3,
         out_specs=[vmem] * 3,
@@ -385,7 +420,7 @@
         ],
         compiler_params=pltpu.CompilerParams(
             collective_id=0, has_side_effects=True,
-            vmem_limit_bytes=60 * 1024 * 1024,
+            vmem_limit_bytes=48 * 1024 * 1024,
         ),
         cost_estimate=pl.CostEstimate(
             flops=6 * rows * D * ff, bytes_accessed=4 * (2 * rows * ff + rows * dx + S * ff),

time: 123 us -> 125 us (1.016)
  no operation moved by 1% of the time
where the time goes in v3:
time: 125 us
  Pallas kernels  118 us (94%)
  local copies, waits for them, and re-layouts  5.57 us (4%)
    pallas_call x1, Pallas kernels, on_device(): pl.pallas_call(functools.partial(kernel, n, peers), out_shape=[pltpu.VMEM...  118 us
    unnamed x7, local copies, waits for them, and re-layouts  5.57 us

profile of v3, /device:TPU:0, one launch (start us, length us, event | category | flops | bytes accessed | tf_op | source)
XLA Modules:
  0.0 124.7 jit_solution(2523165146370365488)
XLA Ops:
  0.6 0.0 copy-start
  0.6 1.4 %copy-done = bf16[512,1536]{1,0:T(8,128)(2,1)S(1)} copy-done((bf16[512,1536]{1,0:T(8,128)(2,1)S(1)}, bf16[512,1536]{1,0:T(8,128)(2,1)}, u32[]{:S(2)}) %copy-start) | copy-done | bytes 1572888
  2.0 0.0 copy-start.1
  2.0 1.1 copy-done.1
  3.1 118.5 %shard_map.58 = (bf16[512,1536]{1,0:T(8,128)(2,1)S(1)}, bf16[512,1536]{1,0:T(8,128)(2,1)S(1)}, bf16[192,1536]{1,0:T(8,128)(2,1)S(1)}) custom-call(bf16[192,1536]{1,0:T(8,128)(2,1)S(1)} %copy-done.1, bf16[512,1536]{1,0:T(8,128)(2,1)S(1)} %copy-done, bf16[512,1536]{1,0:T(8,128)(2,1)} %cot_hbm.1), custom_call_target="tpu_custom_call" | custom-call | flops 14495514624 | bytes 10616832 | tf_op jit(solution)/shard_map/pallas_call | solution.py:392
  121.6 1.1 copy.9
  122.7 0.8 copy.11
  123.5 1.1 copy.10
Async XLA Ops:
  0.6 1.4 %copy-start = (bf16[512,1536]{1,0:T(8,128)(2,1)S(1)}, bf16[512,1536]{1,0:T(8,128)(2,1)}, u32[]{:S(2)}) copy-start(bf16[512,1536]{1,0:T(8,128)(2,1)} %tok_hbm.1) | copy-start | bytes 4718596
  2.0 1.1 copy-start.1

commit v4 on v3

--- a/solution.py
+++ b/solution.py
@@ -13,7 +13,8 @@
 DIRS = 2
 TILE = 256
 SPLIT = 2
-RS_LAG = 3
+AG_LAG = 1
+RS_LAG = 2
 ROOT = 0.7978845608028654
 
 
@@ -33,8 +34,6 @@
     halves = rows // TILE
     ntile = gcols // TILE
     units = halves * ntile
-    ag_lag = max(2, 3 * n // 8)
-    last = 2 * ag_lag - 1
     sr = S // SPLIT
 
     dp = lax.axis_index("dp")
@@ -55,12 +54,16 @@
     def peer(t):
         return {"tensor": lax.rem(x + t, peers)}
 
-    w_load = pltpu.make_async_copy(
-        w_hbm, w_all.at[pl.ds(pl.multiple_of(dp * S, 16), S), :], load_sem.at[0])
+    w_loads = [
+        pltpu.make_async_copy(
+            w_hbm.at[:, pl.ds(k * qcols, qcols)],
+            w_all.at[k, pl.ds(pl.multiple_of(dp * S, 16), S)], load_sem.at[2 + k])
+        for k in range(GROUPS * DIRS)]
     tok_load = pltpu.make_async_copy(
-        tok_hbm, tok.at[:, pl.ds(pl.multiple_of(x * dx, 128), dx)], load_sem.at[1])
-    cot_load = pltpu.make_async_copy(cot_hbm, cot, load_sem.at[2])
-    w_load.start()
+        tok_hbm, tok.at[:, pl.ds(pl.multiple_of(x * dx, 128), dx)], load_sem.at[0])
+    cot_load = pltpu.make_async_copy(cot_hbm, cot, load_sem.at[1])
+    for load in w_loads:
+        load.start()
     tok_load.start()
     cot_load.start()
 
@@ -77,8 +80,7 @@
 
     def w_piece(g, d, pos, core, r):
         owner = chip_at(pos) * 2 + core
-        return w_all.at[pl.ds(pl.multiple_of(owner * S + r * sr, 16), sr),
-                        pl.ds(g * gcols + d * qcols, qcols)]
+        return w_all.at[g * DIRS + d, pl.ds(pl.multiple_of(owner * S + r * sr, 16), sr)]
 
     def sem_at(g, d, h, r):
         return ((g * DIRS + d) * SPLIT + r) * n + h
@@ -115,7 +117,8 @@
             for d in range(DIRS):
                 ag_mate(g, d, 0, r, c).start()
 
-    w_load.wait()
+    for load in w_loads:
+        load.wait()
     ag_start(0)
     tok_load.wait()
     for m in range(halves):
@@ -134,7 +137,8 @@
         m = lax.div(u, ntile)
         rsl = pl.ds(pl.multiple_of(m * TILE, TILE), TILE)
         csl = pl.ds(pl.multiple_of(g * gcols + lax.rem(u, ntile) * TILE, TILE), TILE)
-        v = jnp.dot(tok[rsl, :], w_all[:, csl], preferred_element_type=F32)
+        v = jnp.dot(tok[rsl, :], w_all[g * DIRS + lax.rem(u, ntile)],
+                    preferred_element_type=F32)
         sq = v * v
         th = jnp.tanh(ROOT * v * (1.0 + 0.044715 * sq))
         half = 0.5 * (1.0 + th)
@@ -220,20 +224,29 @@
         for t in range(1, peers):
             tok_in(t, m).wait_recv()
 
-    @pl.loop(0, n - 1 + 2 * ag_lag)
+    def x_block(owner, b):
+        at = pl.ds(pl.multiple_of(owner * dx + b * xcols, 128), xcols)
+        rows_of_w = jnp.concatenate(
+            [w_all[k, at, :] for k in range(GROUPS * DIRS)], axis=1)
+        return lax.dot_general(
+            pg[...], rows_of_w, (((1,), (1,)), ((), ())),
+            preferred_element_type=F32).astype(BF16)
+
+    def x_copy(k):
+        return remote(xsend.at[k], xrecv.at[k], x_s.at[k], x_r.at[k],
+                      peer(lax.div(k, nb) + 1))
+
+    away = (peers - 1) * nb
+
+    def ready(g):
+        return n - 1 + g * RS_LAG
+
+    done = ready(GROUPS)
+
+    @pl.loop(0, done + n)
     def _(s):
-        late = s - (n - 1)
-
-        @pl.when(late == last)
-        def _():
-            for d in range(DIRS):
-                make_part(0, d, 0)
-            combine(0, 0)
-            for d in range(DIRS):
-                make_part(0, d, 1)
-
         for g in range(GROUPS):
-            h = s - g * ag_lag
+            h = s - g * AG_LAG
 
             @pl.when((h >= 0) & (h < n - 1))
             def _():
@@ -248,87 +261,51 @@
                         ag_mate(g, d, h + 1, r, c).start()
 
             if g + 1 < GROUPS:
-                @pl.when(h == ag_lag - 1)
+                @pl.when(h == AG_LAG - 1)
                 def _():
                     ag_start(g + 1)
 
-        @pl.when(late < 0)
+        @pl.when(s < n - 1)
         def _():
             @pl.loop(*spread(strips, s, n - 1))
             def _(k):
                 for m in range(halves):
                     flip(m, x * dx + k * 128)
 
-        @pl.when(late == 0)
-        def _():
-            wait_mates(0)
-            await_tokens(0)
-
-        @pl.when((late >= 0) & (late < ag_lag))
-        def _():
-            @pl.loop(*spread(units, late, ag_lag))
-            def _(u):
-                @pl.when(u == ntile)
+        for g in range(GROUPS):
+            i = s - ready(g)
+            h = i - RS_LAG
+
+            @pl.when((h >= 0) & (h < n))
+            def _():
+                combine(g, h)
+
+            @pl.when((i >= 0) & (i < RS_LAG))
+            def _():
+                @pl.when(i == 0)
                 def _():
-                    await_tokens(1)
-
-                activate(0, u)
-
-            @pl.loop(*spread(others, late, ag_lag))
-            def _(k):
-                flip_other(0, k)
-
-        @pl.when(late == ag_lag)
-        def _():
-            wait_mates(1)
-
-        @pl.when((late >= ag_lag) & (late < last))
-        def _():
-            @pl.loop(*spread(others, late - ag_lag, ag_lag - 1))
-            def _(k):
-                flip_other(1, k)
-
-            @pl.loop(*spread(units, late - ag_lag, ag_lag - 1))
-            def _(u):
-                activate(1, u)
-
-    def x_block(owner, b):
-        at = pl.ds(pl.multiple_of(owner * dx + b * xcols, 128), xcols)
-        return lax.dot_general(
-            pg[...], w_all[at, :], (((1,), (1,)), ((), ())),
-            preferred_element_type=F32).astype(BF16)
-
-    def x_copy(k):
-        return remote(xsend.at[k], xrecv.at[k], x_s.at[k], x_r.at[k],
-                      peer(lax.div(k, nb) + 1))
-
-    away = (peers - 1) * nb
-
-    @pl.loop(1, n + 2 * RS_LAG)
-    def _(s):
-        @pl.when(s == 1)
-        def _():
-            wait_mates(2)
-
-        for g in range(GROUPS):
-            h = s - g * RS_LAG
-
-            @pl.when((h >= 0) & (h < n))
-            def _():
-                combine(g, h)
+                    wait_mates(g)
+
+                if g == 0:
+                    for m in range(halves):
+                        @pl.when(i == m * RS_LAG // halves)
+                        def _():
+                            await_tokens(m)
+
+                            @pl.loop(0, others)
+                            def _(k):
+                                flip_other(m, k)
+
+                @pl.loop(*spread(units, i, RS_LAG))
+                def _(u):
+                    activate(g, u)
 
             @pl.when((h >= -1) & (h < n - 1))
             def _():
                 for d in range(DIRS):
                     make_part(g, d, h + 1)
 
-        @pl.when(s < 3)
-        def _():
-            @pl.loop(*spread(units, s - 1, 2))
-            def _(u):
-                activate(2, u)
-
-        e = s - 3
+        e = s - done
 
         @pl.when((e >= 0) & (e < 2))
         def _():
@@ -399,7 +376,7 @@
         in_specs=[any_spec] * 3,
         out_specs=[vmem] * 3,
         scratch_shapes=[
-            pltpu.VMEM((D, ff), BF16),
+            pltpu.VMEM((GROUPS * DIRS, D, qcols), BF16),
             pltpu.VMEM((rows, D), BF16),
             pltpu.VMEM((D, rows), BF16),
             pltpu.VMEM((rows, ff), BF16),
@@ -411,7 +388,7 @@
             pltpu.VMEM((slots, S, qcols), BF16),
             pltpu.VMEM((nx, rows, xcols), BF16),
             pltpu.VMEM((nx, rows, xcols), BF16),
-            dma((3,)),
+            dma((2 + GROUPS * DIRS,)),
             dma(((peers - 1) * halves,)), dma(((peers - 1) * halves,)),
             dma((slots * SPLIT,)), dma((slots * SPLIT,)),
             dma((slots * SPLIT,)), dma((slots * SPLIT,)),
@@ -420,7 +397,7 @@
         ],
         compiler_params=pltpu.CompilerParams(
             collective_id=0, has_side_effects=True,
-            vmem_limit_bytes=48 * 1024 * 1024,
+            vmem_limit_bytes=60 * 1024 * 1024,
         ),
         cost_estimate=pl.CostEstimate(
             flops=6 * rows * D * ff, bytes_accessed=4 * (2 * rows * ff + rows * dx + S * ff),

time: 125 us -> 124 us (level)
  local copies, waits for them, and re-layouts: 5.57 us -> 3.1 us
  Pallas kernels: 118 us -> 120 us
    unnamed x7 -> x3, local copies, waits for them, and re-layouts: 5.57 us -> 3.1 us
    pallas_call x1, Pallas kernels: 118 us -> 120 us  [on_device(): pl.pallas_call(functools.partial(kernel, n, peers), out_shape=[pltpu.VMEM...]
where the time goes in v4:
time: 124 us
  Pallas kernels  120 us (97%)
  local copies, waits for them, and re-layouts  3.1 us (2%)
    pallas_call x1, Pallas kernels, on_device(): pl.pallas_call(functools.partial(kernel, n, peers), out_shape=[pltpu.VMEM...  120 us
    unnamed x3, local copies, waits for them, and re-layouts  3.1 us

profile of v4, /device:TPU:0, one launch (start us, length us, event | category | flops | bytes accessed | tf_op | source)
XLA Modules:
  0.0 123.7 jit_solution(7664571011793963949)
XLA Ops:
  0.6 120.0 %shard_map.58 = (bf16[512,1536]{1,0:T(8,128)(2,1)S(1)}, bf16[512,1536]{1,0:T(8,128)(2,1)S(1)}, bf16[192,1536]{1,0:T(8,128)(2,1)S(1)}) custom-call(bf16[192,1536]{1,0:T(8,128)(2,1)} %w_hbm.1, bf16[512,1536]{1,0:T(8,128)(2,1)} %tok_hbm.1, bf16[512,1536]{1,0:T(8,128)(2,1)} %cot_hbm.1), custom_call_target="tpu_custom_call" | custom-call | flops 14495514624 | bytes 10616832 | tf_op jit(solution)/shard_map/pallas_call | solution.py:369
  120.6 1.1 copy.9
  121.8 0.8 copy.11
  122.6 1.1 copy.10

commit v5 on v4

--- a/solution.py
+++ b/solution.py
@@ -13,8 +13,9 @@
 DIRS = 2
 TILE = 256
 SPLIT = 2
-AG_LAG = 1
-RS_LAG = 2
+AG_LAG = 2
+READY = (-1, 1, 3)
+REDUCE = (1, 3, 4)
 ROOT = 0.7978845608028654
 
 
@@ -238,10 +239,7 @@
 
     away = (peers - 1) * nb
 
-    def ready(g):
-        return n - 1 + g * RS_LAG
-
-    done = ready(GROUPS)
+    done = n + REDUCE[-1]
 
     @pl.loop(0, done + n)
     def _(s):
@@ -273,14 +271,15 @@
                     flip(m, x * dx + k * 128)
 
         for g in range(GROUPS):
-            i = s - ready(g)
-            h = i - RS_LAG
+            i = s - n - READY[g]
+            h = s - n - REDUCE[g]
+            span = REDUCE[g] - READY[g]
 
             @pl.when((h >= 0) & (h < n))
             def _():
                 combine(g, h)
 
-            @pl.when((i >= 0) & (i < RS_LAG))
+            @pl.when((i >= 0) & (i < span))
             def _():
                 @pl.when(i == 0)
                 def _():
@@ -288,7 +287,7 @@
 
                 if g == 0:
                     for m in range(halves):
-                        @pl.when(i == m * RS_LAG // halves)
+                        @pl.when(i == m * span // halves)
                         def _():
                             await_tokens(m)
 
@@ -296,7 +295,7 @@
                             def _(k):
                                 flip_other(m, k)
 
-                @pl.loop(*spread(units, i, RS_LAG))
+                @pl.loop(*spread(units, i, span))
                 def _(u):
                     activate(g, u)
 
@@ -307,9 +306,9 @@
 
         e = s - done
 
-        @pl.when((e >= 0) & (e < 2))
-        def _():
-            @pl.loop(*spread(away, e, 2))
+        @pl.when(e == 0)
+        def _():
+            @pl.loop(0, away)
             def _(k):
                 t = lax.div(k, nb) + 1
                 xsend[k] = x_block(lax.rem(x + t, peers), lax.rem(k, nb))

time: 124 us -> 118 us (0.952)
  Pallas kernels: 120 us -> 114 us
    pallas_call x1, Pallas kernels: 120 us -> 114 us  [on_device(): pl.pallas_call(functools.partial(kernel, n, peers), out_shape=[pltpu.VMEM...]
where the time goes in v5:
time: 118 us
  Pallas kernels  114 us (97%)
  local copies, waits for them, and re-layouts  3.1 us (3%)
    pallas_call x1, Pallas kernels, on_device(): pl.pallas_call(functools.partial(kernel, n, peers), out_shape=[pltpu.VMEM...  114 us
    unnamed x3, local copies, waits for them, and re-layouts  3.1 us

profile of v5, /device:TPU:0, one launch (start us, length us, event | category | flops | bytes accessed | tf_op | source)
XLA Modules:
  0.0 117.5 jit_solution(5184369728172030157)
XLA Ops:
  0.6 113.8 %shard_map.58 = (bf16[512,1536]{1,0:T(8,128)(2,1)S(1)}, bf16[512,1536]{1,0:T(8,128)(2,1)S(1)}, bf16[192,1536]{1,0:T(8,128)(2,1)S(1)}) custom-call(bf16[192,1536]{1,0:T(8,128)(2,1)} %w_hbm.1, bf16[512,1536]{1,0:T(8,128)(2,1)} %tok_hbm.1, bf16[512,1536]{1,0:T(8,128)(2,1)} %cot_hbm.1), custom_call_target="tpu_custom_call" | custom-call | flops 14495514624 | bytes 10616832 | tf_op jit(solution)/shard_map/pallas_call | solution.py:368
  114.4 1.1 copy.9
  115.5 0.8 copy.11
  116.4 1.1 copy.10

commit v6 on v5

--- a/solution.py
+++ b/solution.py
@@ -320,6 +320,27 @@
             def _(b):
                 xg[:, pl.ds(pl.multiple_of(b * xcols, 128), xcols)] = x_block(x, b)
 
+        @pl.when((e >= 0) & (e < n))
+        def _():
+            for g in range(GROUPS):
+                for d in range(DIRS):
+                    for r in range(SPLIT):
+                        ag_mate(g, d, e, r, c).wait_send()
+
+                        @pl.when(e < n - 1)
+                        def _():
+                            ag_ring(g, d, e, r).wait_send()
+
+        for g in range(GROUPS):
+            h = s - n - REDUCE[g]
+
+            @pl.when((h >= 2) & (h < n))
+            def _():
+                for d in range(DIRS):
+                    rs_mate(g, d, h - 2).wait_send()
+                    for r in range(SPLIT):
+                        rs_ring(g, d, h - 2, r).wait_send()
+
     @pl.loop(0, nb)
     def _(b):
         at = pl.ds(pl.multiple_of(b * xcols, 128), xcols)
@@ -330,18 +351,12 @@
             total = total + xrecv[k].astype(F32)
         xg[:, at] = total.astype(BF16)
 
-    @pl.loop(0, n)
-    def _(h):
-        for g in range(GROUPS):
-            for d in range(DIRS):
+    for g in range(GROUPS):
+        for d in range(DIRS):
+            for h in (n - 2, n - 1):
                 rs_mate(g, d, h).wait_send()
-                for r in range(SPLIT):
-                    ag_mate(g, d, h, r, c).wait_send()
-
-                    @pl.when(h < n - 1)
-                    def _():
-                        ag_ring(g, d, h, r).wait_send()
-                        rs_ring(g, d, h, r).wait_send()
+            for r in range(SPLIT):
+                rs_ring(g, d, n - 2, r).wait_send()
 
     @pl.loop(0, away)
     def _(k):
@@ -350,6 +365,16 @@
     for m in range(halves):
         for t in range(1, peers):
             tok_copy(t, m).wait_send()
+
+
+def store(*refs):
+    sems = refs[6]
+    copies = [
+        pltpu.make_async_copy(refs[k], refs[3 + k], sems.at[k]) for k in range(3)]
+    for copy in copies:
+        copy.start()
+    for copy in copies:
+        copy.wait()
 
 
 def on_device(n_dp, peers, tokens, w_in, cotangent):
@@ -365,7 +390,7 @@
     vmem = pl.BlockSpec(memory_space=pltpu.VMEM)
     dma = pltpu.SemaphoreType.DMA
     halves = rows // TILE
-    return pl.pallas_call(
+    results = pl.pallas_call(
         functools.partial(kernel, n, peers),
         out_shape=[
             pltpu.VMEM((rows, ff), BF16),
@@ -402,6 +427,17 @@
             flops=6 * rows * D * ff, bytes_accessed=4 * (2 * rows * ff + rows * dx + S * ff),
             transcendentals=rows * ff),
     )(w_in, tokens, cotangent)
+    return pl.pallas_call(
+        store,
+        out_shape=[
+            jax.ShapeDtypeStruct((rows, ff), BF16),
+            jax.ShapeDtypeStruct((rows, dx), BF16),
+            jax.ShapeDtypeStruct((S, ff), BF16),
+        ],
+        in_specs=[vmem] * 3,
+        out_specs=[any_spec] * 3,
+        scratch_shapes=[dma((3,))],
+    )(*results)
 
 
 def solution(mesh):

time: 118 us -> 121 us (1.025)
  Pallas kernels: 114 us -> 117 us
    pallas_call x0 -> x1, Pallas kernels: none -> 3.88 us  [on_device(): pl.pallas_call(store, out_shape=[jax.ShapeDtypeStruct((rows, ff), BF16),...]
    unnamed x3 -> x6, local copies, waits for them, and re-layouts: 3.1 us -> 3.12 us
where the time goes in v6:
time: 121 us
  Pallas kernels  117 us (97%)
  local copies, waits for them, and re-layouts  3.12 us (3%)
    pallas_call x1, Pallas kernels, on_device(): pl.pallas_call(functools.partial(kernel, n, peers), out_shape=[pltpu.VMEM...  113 us
    pallas_call x1, Pallas kernels, on_device(): pl.pallas_call(store, out_shape=[jax.ShapeDtypeStruct((rows, ff), BF16),...  3.88 us
    unnamed x6, local copies, waits for them, and re-layouts  3.12 us

profile of v6, /device:TPU:0, one launch (start us, length us, event | category | flops | bytes accessed | tf_op | source)
XLA Modules:
  0.0 121.1 jit_solution(10276730207573134039)
XLA Ops:
  0.6 113.5 %shard_map.58 = (bf16[512,1536]{1,0:T(8,128)(2,1)S(1)}, bf16[512,1536]{1,0:T(8,128)(2,1)S(1)}, bf16[192,1536]{1,0:T(8,128)(2,1)S(1)}) custom-call(bf16[192,1536]{1,0:T(8,128)(2,1)} %w_hbm.1, bf16[512,1536]{1,0:T(8,128)(2,1)} %tok_hbm.1, bf16[512,1536]{1,0:T(8,128)(2,1)} %cot_hbm.1), custom_call_target="tpu_custom_call" | custom-call | flops 14495514624 | bytes 10616832 | tf_op jit(solution)/shard_map/pallas_call | solution.py:393
  114.1 0.0 copy-start
  114.1 1.2 copy-done
  115.3 0.0 copy-start.1
  115.3 1.2 copy-done.1
  116.4 0.0 copy-start.2
  116.4 0.8 copy-done.2
  117.2 3.9 %shard_map.59 = (bf16[512,1536]{1,0:T(8,128)(2,1)}, bf16[512,1536]{1,0:T(8,128)(2,1)}, bf16[192,1536]{1,0:T(8,128)(2,1)}) custom-call(bf16[512,1536]{1,0:T(8,128)(2,1)} %copy-done, bf16[512,1536]{1,0:T(8,128)(2,1)} %copy-done.1, bf16[192,1536]{1,0:T(8,128)(2,1)} %copy-done.2), custom_call_target="tpu_custom_call" | custom-call | tf_op jit(solution)/shard_map/pallas_call | solution.py:430
Async XLA Ops:
  114.1 1.2 copy-start
  115.3 1.2 copy-start.1
  116.4 0.8 copy-start.2

commit v7 on v6

--- a/solution.py
+++ b/solution.py
@@ -12,7 +12,7 @@
 GROUPS = 3
 DIRS = 2
 TILE = 256
-SPLIT = 2
+SPLIT = 1
 AG_LAG = 2
 READY = (-1, 1, 3)
 REDUCE = (1, 3, 4)
@@ -367,16 +367,6 @@
             tok_copy(t, m).wait_send()
 
 
-def store(*refs):
-    sems = refs[6]
-    copies = [
-        pltpu.make_async_copy(refs[k], refs[3 + k], sems.at[k]) for k in range(3)]
-    for copy in copies:
-        copy.start()
-    for copy in copies:
-        copy.wait()
-
-
 def on_device(n_dp, peers, tokens, w_in, cotangent):
     n = n_dp // 2
     S, ff = w_in.shape
@@ -390,7 +380,7 @@
     vmem = pl.BlockSpec(memory_space=pltpu.VMEM)
     dma = pltpu.SemaphoreType.DMA
     halves = rows // TILE
-    results = pl.pallas_call(
+    return pl.pallas_call(
         functools.partial(kernel, n, peers),
         out_shape=[
             pltpu.VMEM((rows, ff), BF16),
@@ -427,17 +417,6 @@
             flops=6 * rows * D * ff, bytes_accessed=4 * (2 * rows * ff + rows * dx + S * ff),
             transcendentals=rows * ff),
     )(w_in, tokens, cotangent)
-    return pl.pallas_call(
-        store,
-        out_shape=[
-            jax.ShapeDtypeStruct((rows, ff), BF16),
-            jax.ShapeDtypeStruct((rows, dx), BF16),
-            jax.ShapeDtypeStruct((S, ff), BF16),
-        ],
-        in_specs=[vmem] * 3,
-        out_specs=[any_spec] * 3,
-        scratch_shapes=[dma((3,))],
-    )(*results)
 
 
 def solution(mesh):

time: 121 us -> 118 us (0.975)
  Pallas kernels: 117 us -> 114 us
    pallas_call x1 -> x0, Pallas kernels: 3.88 us -> none  [on_device(): pl.pallas_call(store, out_shape=[jax.ShapeDtypeStruct((rows, ff), BF16),...]
    unnamed x6 -> x3, local copies, waits for them, and re-layouts: 3.12 us -> 3.1 us
where the time goes in v7:
time: 118 us
  Pallas kernels  114 us (97%)
  local copies, waits for them, and re-layouts  3.1 us (3%)
    pallas_call x1, Pallas kernels, on_device(): pl.pallas_call(functools.partial(kernel, n, peers), out_shape=[pltpu.VMEM...  114 us
    unnamed x3, local copies, waits for them, and re-layouts  3.1 us

profile of v7, /device:TPU:0, one launch (start us, length us, event | category | flops | bytes accessed | tf_op | source)
XLA Modules:
  0.0 118.0 jit_solution(8301060868521030833)
XLA Ops:
  0.6 114.3 %shard_map.58 = (bf16[512,1536]{1,0:T(8,128)(2,1)S(1)}, bf16[512,1536]{1,0:T(8,128)(2,1)S(1)}, bf16[192,1536]{1,0:T(8,128)(2,1)S(1)}) custom-call(bf16[192,1536]{1,0:T(8,128)(2,1)} %w_hbm.1, bf16[512,1536]{1,0:T(8,128)(2,1)} %tok_hbm.1, bf16[512,1536]{1,0:T(8,128)(2,1)} %cot_hbm.1), custom_call_target="tpu_custom_call" | custom-call | flops 14495514624 | bytes 10616832 | tf_op jit(solution)/shard_map/pallas_call | solution.py:383
  114.9 1.1 copy.9
  116.1 0.8 copy.11
  116.9 1.1 copy.10
